TPU v7x, 32 devices: a whole 2x2x4 slice. The times are simulated.
32 devices in a mesh: az: 4 (over y, x), rad: 8 (over z, core).
Axes of the slice: x: 2, y: 2, z: 4, core: 2. Of those that a mesh axis runs over, the one named last changes fastest.
Arguments:
- field: bfloat16 [256, 4, 1024, 128], P('az', None, 'rad'), may hold values from -6 to 6
- shell_counts: int32 [8], replicated, may hold values from 1 to 128, 512 in all
- op_index: int32 [129], replicated, may hold values from 0 to 1
- radial_ops: bfloat16 [2, 512, 512], replicated, may hold values from -0.25 to 0.25
Outputs:
- result: bfloat16 [256, 4, 128, 512], P('az', None, 'rad')
Inputs may be any that keep to these rules, and one draw needn't show every extreme that they name: Rad index j holds shell_counts[j] radial cells in its first slots, shells in order from the axis outward; its other slots hold no data; the counts sum to 512 and the largest equals 128. op_index[m] names the radial operator of azimuthal mode number m.
All inputs are finite; a program needn't handle non-finite values.
Results may differ from a plain program's by a relative error of at most 0.0059.
Values may be sent and summed in bfloat16 or wider, within the bound.
A program may use at most 192 MiB of HBM per device.

v0:
```python
import math

import jax
import jax.numpy as jnp
from jax import lax
from jax.sharding import PartitionSpec as P


def make_table(length):
    index = jnp.arange(length, dtype=jnp.int32)
    product = index[:, None] * index[None, :] % length
    angle = product.astype(jnp.float32) * (2.0 * math.pi / length)
    return ((jnp.cos(angle) + jnp.sin(angle)) * (1.0 / math.sqrt(length))).astype(jnp.bfloat16)


def slot_index(counts, capacity, radial):
    starts = jnp.cumsum(counts) - counts
    rows = jnp.arange(radial, dtype=jnp.int32)
    owner = jnp.sum((starts[None, :] <= rows[:, None]).astype(jnp.int32), axis=1) - 1
    return owner * capacity + rows - jnp.take(starts, owner)


def to_planes(values):
    return lax.all_to_all(values, "az", split_axis=3, concat_axis=0, tiled=True)


def to_modes(values):
    return lax.all_to_all(values, "az", split_axis=0, concat_axis=3, tiled=True)


def regroup_shells(values):
    return lax.all_to_all(values, "rad", split_axis=3, concat_axis=2, tiled=True)


def transform(cas_table, values):
    shape = values.shape
    flat = jnp.dot(cas_table, values.reshape(shape[0], -1), preferred_element_type=jnp.float32)
    return flat.astype(jnp.bfloat16).reshape(shape)


def per_device(field, shell_counts, op_index, radial_ops):
    planes = field.shape[0]
    slots_dev = field.shape[2]
    az_count = lax.axis_size("az")
    comps_all = planes * az_count
    radial = radial_ops.shape[1]
    row_slot = slot_index(shell_counts, slots_dev, radial)
    cas_table = make_table(comps_all)
    az_block = lax.axis_index("az")
    comp_ids = az_block * planes + jnp.arange(planes, dtype=jnp.int32)
    mode_ids = jnp.minimum(comp_ids, comps_all - comp_ids)
    chosen = jnp.take(radial_ops, jnp.take(op_index, mode_ids), axis=0)
    gathered = to_planes(field)
    spectra = transform(cas_table, gathered)
    returned = to_modes(spectra)
    slab_data = regroup_shells(returned)
    packed = jnp.take(slab_data, row_slot, axis=2)
    result = jnp.einsum("crs,cfsx->cfxr", chosen, packed, preferred_element_type=jnp.float32)
    return result.astype(jnp.bfloat16)


def solution(mesh):
    return jax.shard_map(
        per_device,
        mesh=mesh,
        in_specs=(P("az", None, "rad", None), P(), P(), P()),
        out_specs=P("az", None, "rad", None),
        check_vma=False,
    )
```

profile of v0, /device:TPU:0, one launch (start us, length us, event | category | flops | bytes accessed | tf_op | source)
XLA Modules:
  0.0 638.9 jit_solution(9558354405037593036)
XLA Ops:
  0.0 0.0 copy-start
  0.0 14.7 %copy.43 = bf16[64,4,128,128]{2,1,0,3:T(4,128)(2,1)} copy(bf16[64,4,128,128]{3,2,1,0:T(8,128)(2,1)} %param.4) | data formatting | bytes 16777216 | tf_op args[0]
  14.7 101.8 %all_to_all.51 = bf16[64,4,128,128]{2,1,0,3:T(4,128)(2,1)} all-to-all(bf16[64,4,128,128]{2,1,0,3:T(4,128)(2,1)} %copy.43), channel_id=1, replica_groups=mesh['az'=4,'rad'=8] {'az'}, dimensions={3} | all-to-all | bytes 16777216 | tf_op jit(solution)/shard_map/all_to_all | solution.py:24
  116.5 16.3 %copy.44 = bf16[64,4,128,128]{2,3,1,0:T(8,128)(2,1)} copy(bf16[64,4,128,128]{2,1,0,3:T(4,128)(2,1)} %all_to_all.51) | data formatting | bytes 16777216 | tf_op jit(solution)/shard_map/all_to_all | solution.py:24
  132.8 29.3 %copy.45 = bf16[4,64,4,128,32]{1,0,4,3,2:T(4,128)(2,1)} copy(bf16[4,64,4,128,32]{3,4,0,2,1:T(8,128)(2,1)} %bitcast.50) | data formatting | bytes 16777216 | tf_op jit(solution)/shard_map/all_to_all | solution.py:24
  162.1 24.4 %reshape.169 = bf16[256,16384]{0,1:T(8,128)(2,1)} reshape(bf16[4,64,4,128,32]{1,0,4,3,2:T(4,128)(2,1)} %copy.45) | data formatting | bytes 16777216 | tf_op jit(solution)/shard_map/reshape | solution.py:37
  186.5 11.7 %convolution_convert_fusion = bf16[256,16384]{1,0:T(8,128)(2,1)} fusion(bf16[256,16384]{0,1:T(8,128)(2,1)} %reshape.169), kind=kOutput, calls=%fused_computation.7 | convolution fusion | flops 2152792064 | bytes 16777216 | tf_op jit(solution)/shard_map/dot_general | solution.py:37
  198.1 11.9 %copy.46 = bf16[256,16384]{0,1:T(8,128)(2,1)} copy(bf16[256,16384]{1,0:T(8,128)(2,1)} %convolution_convert_fusion) | data formatting | bytes 16777216 | tf_op jit(solution)/shard_map/convert_element_type | solution.py:38
  210.0 16.9 %copy.47 = bf16[256,4,128,32]{2,3,1,0:T(8,128)(2,1)} copy(bf16[256,4,128,32]{0,3,2,1:T(8,128)(2,1)} %bitcast.52) | data formatting | bytes 16777216 | tf_op jit(solution)/shard_map/reshape | solution.py:38
  226.9 99.6 %all_to_all.52 = bf16[256,4,128,32]{2,3,1,0:T(8,128)(2,1)} all-to-all(bf16[256,4,128,32]{2,3,1,0:T(8,128)(2,1)} %copy.47), channel_id=1, replica_groups=mesh['az'=4,'rad'=8] {'az'}, dimensions={0} | all-to-all | bytes 16777216 | tf_op jit(solution)/shard_map/all_to_all | solution.py:28
  326.6 9.2 %copy.48 = bf16[64,4,128,4,32]{2,4,3,1,0:T(8,128)(2,1)} copy(bf16[64,4,128,4,32]{2,4,1,0,3:T(8,128)(2,1)} %bitcast.53) | data formatting | bytes 16777216 | tf_op jit(solution)/shard_map/all_to_all | solution.py:28
  335.8 8.4 %copy.49 = bf16[64,4,128,128]{2,1,0,3:T(4,128)(2,1)} copy(bf16[64,4,128,128]{2,3,1,0:T(8,128)(2,1)} %bitcast.54) | data formatting | bytes 16777216 | tf_op jit(solution)/shard_map/all_to_all | solution.py:28
  344.2 0.0 copy-start.3
  344.2 0.0 copy-start.2
  344.2 5.3 all-to-all-start.2
  349.5 0.0 copy-done.3
  349.6 0.2 reduce-window.9
  349.8 0.0 copy-done.2
  349.8 0.8 gather_fusion.1
  350.6 0.0 copy-done
  350.6 12.2 %gather_fusion.2 = bf16[64,512,512]{2,1,0:T(8,128)(2,1)} fusion(bf16[2,512,512]{2,1,0:T(8,128)(2,1)S(1)} %copy-done, s32[1024]{0:T(1024)S(1)} %pad_clamp_fusion), kind=kCustom, calls=%fused_computation.2 | custom fusion | bytes 67109120 | tf_op jit(solution)/shard_map/jit(_take)/gather | solution.py:52
  362.8 0.7 fusion.28
  363.5 0.1 convert_reduce_fusion
  363.6 4.4 compare_select_fusion.2
  367.9 0.7 compare_and_fusion.1
  368.7 164.8 %all-to-all-done.2 = bf16[64,4,128,128]{2,1,0,3:T(4,128)(2,1)} async-done(((bf16[64,4,128,128]{2,1,0,3:T(4,128)(2,1)}), bf16[64,4,128,128]{2,1,0,3:T(4,128)(2,1)}, u32[]{:S(2)}, u32[]{:S(2)}) %all-to-all-start.2) | async-done | bytes 8388640 | tf_op jit(solution)/shard_map/all_to_all | solution.py:32
  533.4 16.3 %copy.50 = bf16[64,4,128,128]{2,3,1,0:T(8,128)(2,1)} copy(bf16[64,4,128,128]{2,1,0,3:T(4,128)(2,1)} %all-to-all-done.2) | data formatting | bytes 16777216 | tf_op jit(solution)/shard_map/all_to_all | solution.py:32
  549.7 23.9 %copy.55 = bf16[64,4,8,128,16]{0,4,3,2,1:T(8,128)(2,1)} copy(bf16[64,4,8,128,16]{3,4,2,1,0:T(8,128)(2,1)} %bitcast.51) | data formatting | bytes 16777216 | tf_op jit(solution)/shard_map/all_to_all | solution.py:32
  573.6 26.2 %gather_fusion = bf16[512,64,4,16]{1,3,2,0:T(8,128)(2,1)} fusion(bf16[64,4,1024,16]{0,3,2,1:T(8,128)(2,1)} %bitcast.49, s32[1024]{0:T(1024)S(1)} %pad_clamp_fusion.2), kind=kCustom, calls=%fused_computation | custom fusion | bytes 8390656 | tf_op jit(solution)/shard_map/jit(_take)/gather | solution.py:57
  599.9 7.6 %select_bitcast_fusion = bf16[64,4,512,16]{0,3,1,2:T(8,128)(2,1)} fusion(bf16[512,64,4,16]{1,3,2,0:T(8,128)(2,1)} %gather_fusion, pred[512]{0:T(512)(128)(4,1)S(1)} %get-tuple-element.5), kind=kLoop, calls=%fused_computation.9 | loop fusion | flops 2097152 | bytes 8389120 | tf_op jit(solution)/shard_map/jit(_take)/select_n | solution.py:57
  607.5 12.0 %copy.53 = bf16[64,4,512,16]{2,3,1,0:T(8,128)(2,1)} copy(bf16[64,4,512,16]{0,3,1,2:T(8,128)(2,1)} %select_bitcast_fusion) | data formatting | bytes 8388608 | tf_op jit(solution)/shard_map/jit(_take)/select_n | solution.py:57
  619.5 0.0 copy-start.1
  619.5 19.0 %fusion.5 = bf16[64,4,16,512]{3,2,1,0:T(8,128)(2,1)} fusion(bf16[64,4,512,16]{2,3,1,0:T(8,128)(2,1)} %copy.53, bf16[64,512,512]{2,1,0:T(8,128)(2,1)} %gather_fusion.2, pred[64]{0:T(512)(128)(4,1)S(1)} %compare_and_fusion), kind=kOutput, calls=%fused_computation.10 | convolution fusion | flops 2166358016 | bytes 41943104 | tf_op jit(solution)/shard_map/crs,cfsx->cfxr/dot_general | solution.py:58
  638.5 0.0 copy-done.1
  (10 shorter events, 0.1 us)
Async XLA Ops:
  0.0 350.6 %copy-start = (bf16[2,512,512]{2,1,0:T(8,128)(2,1)S(1)}, bf16[2,512,512]{2,1,0:T(8,128)(2,1)}, u32[]{:S(2)}) copy-start(bf16[2,512,512]{2,1,0:T(8,128)(2,1)} %param.7) | copy-start | bytes 3145732
  344.2 5.3 copy-start.3
  344.2 5.5 copy-start.2
  344.2 189.2 %all-to-all-start.2 = ((bf16[64,4,128,128]{2,1,0,3:T(4,128)(2,1)}), bf16[64,4,128,128]{2,1,0,3:T(4,128)(2,1)}, u32[]{:S(2)}, u32[]{:S(2)}) async-start(bf16[64,4,128,128]{2,1,0,3:T(4,128)(2,1)} %copy.49), calls=%async_computation.2 | async-start | bytes 16777216 | tf_op jit(solution)/shard_map/all_to_all | solution.py:32
  619.5 19.0 %copy-start.1 = (bf16[2,512,512]{2,1,0:T(8,128)(2,1)S(1)}, bf16[2,512,512]{2,1,0:T(8,128)(2,1)}, u32[]{:S(2)}) copy-start(bf16[2,512,512]{2,1,0:T(8,128)(2,1)} %param.7) | copy-start | bytes 3145732
where the time goes:
time: 651 us; the launch traced here: 639 us
  local copies, waits for them, and re-layouts  223 us (34%)
  blocking collectives  201 us (31%)
  waiting for transfers between devices  165 us (25%)
  matrix products  30.6 us (5%)
  other arithmetic  13 us (2%)
    all_to_all x1, waiting for transfers between devices, regroup_shells(): lax.all_to_all(values, 'rad', split_axis=3, concat_axis=2, tiled=True)  165 us
    all_to_all x1, blocking collectives, to_planes(): return lax.all_to_all(values, 'az', split_axis=3, concat_axis=0, tiled=True)  102 us
    all_to_all x1, blocking collectives, to_modes(): return lax.all_to_all(values, 'az', split_axis=0, concat_axis=3, tiled=True)  99.6 us
    all_to_all x2, local copies, waits for them, and re-layouts, to_planes(): return lax.all_to_all(values, 'az', split_axis=3, concat_axis=0, tiled=True)  45.6 us
    all_to_all x2, local copies, waits for them, and re-layouts, regroup_shells(): lax.all_to_all(values, 'rad', split_axis=3, concat_axis=2, tiled=True)  40.2 us
    gather x1, local copies, waits for them, and re-layouts, per_device(): packed = jnp.take(slab_data, row_slot, axis=2)  26.2 us
    reshape x1, local copies, waits for them, and re-layouts, transform(): values.reshape(shape[0], -1)  24.4 us
    dot_general x1, matrix products, per_device(): jnp.einsum('crs,cfsx->cfxr', chosen, packed, preferred_element_type=jnp.f...  19 us
  transfers between devices with their start and end apart: 1, of which 1 were waited for; matrix products, arithmetic and copies ran while one was open for 3% of the time, Pallas kernels for 0%

commit v1 on v0

--- a/solution.py
+++ b/solution.py
@@ -1,9 +1,16 @@
+import functools
 import math
 
 import jax
 import jax.numpy as jnp
 from jax import lax
+from jax.experimental import pallas as pl
+from jax.experimental.pallas import tpu as pltpu
 from jax.sharding import PartitionSpec as P
+
+MESH = pl.DeviceIdType.MESH
+VMEM_LIMIT = 48 << 20
+AHEAD = 2
 
 
 def make_table(length):
@@ -38,18 +45,8 @@
     return flat.astype(jnp.bfloat16).reshape(shape)
 
 
-def per_device(field, shell_counts, op_index, radial_ops):
-    planes = field.shape[0]
-    slots_dev = field.shape[2]
-    az_count = lax.axis_size("az")
-    comps_all = planes * az_count
-    radial = radial_ops.shape[1]
-    row_slot = slot_index(shell_counts, slots_dev, radial)
-    cas_table = make_table(comps_all)
-    az_block = lax.axis_index("az")
-    comp_ids = az_block * planes + jnp.arange(planes, dtype=jnp.int32)
-    mode_ids = jnp.minimum(comp_ids, comps_all - comp_ids)
-    chosen = jnp.take(radial_ops, jnp.take(op_index, mode_ids), axis=0)
+def plain_path(field, row_slot, cas_table, chosen_ids, radial_ops):
+    chosen = jnp.take(radial_ops, chosen_ids, axis=0)
     gathered = to_planes(field)
     spectra = transform(cas_table, gathered)
     returned = to_modes(spectra)
@@ -57,6 +54,207 @@
     packed = jnp.take(slab_data, row_slot, axis=2)
     result = jnp.einsum("crs,cfsx->cfxr", chosen, packed, preferred_element_type=jnp.float32)
     return result.astype(jnp.bfloat16)
+
+
+def lay_out_kernel(field_ref, out_ref):
+    turned = jnp.swapaxes(field_ref[:, 0], 1, 2)
+    by_cell = jnp.swapaxes(turned, 0, 1)
+    slabs, _, slab, block, slots = out_ref.shape
+    out_ref[:, 0] = by_cell.reshape(slabs, slab, block, slots)
+
+
+def lay_out(field, n_rad):
+    planes, fields, slots, cells = field.shape
+    slab = cells // n_rad
+    block = 16
+    return pl.pallas_call(
+        lay_out_kernel,
+        grid=(fields, planes // block),
+        in_specs=[pl.BlockSpec((block, 1, slots, cells), lambda f, a: (a, f, 0, 0))],
+        out_specs=pl.BlockSpec((n_rad, 1, slab, block, slots), lambda f, a: (0, f, 0, a, 0)),
+        out_shape=jax.ShapeDtypeStruct((n_rad, fields, slab, planes, slots), field.dtype),
+        compiler_params=pltpu.CompilerParams(vmem_limit_bytes=VMEM_LIMIT),
+    )(field)
+
+
+def exchange_kernel(n_az, n_rad, cells_ref, pack_ref, cas_ref, out_ref, shells, packed, planes_in,
+                    spectra, rad_send, rad_recv, az_send, az_recv, back_send, back_recv, local_sem):
+    az, rad = lax.axis_index("az"), lax.axis_index("rad")
+    _, fields, slab, planes, slots = shells.shape
+    block = packed.shape[4]
+
+    barrier = pltpu.get_barrier_semaphore()
+    for step in range(1, n_rad):
+        pl.semaphore_signal(barrier, inc=1, device_id=(az, lax.rem(rad + step, n_rad)), device_id_type=MESH)
+    for step in range(1, n_az):
+        pl.semaphore_signal(barrier, inc=1, device_id=(lax.rem(az + step, n_az), rad), device_id_type=MESH)
+    pl.semaphore_wait(barrier, n_rad + n_az - 2)
+
+    def rad_copy(f, step):
+        other = lax.rem(rad + step, n_rad)
+        return pltpu.make_async_remote_copy(
+            src_ref=cells_ref.at[other, f], dst_ref=shells.at[rad, f],
+            send_sem=rad_send.at[f, step], recv_sem=rad_recv.at[f, step],
+            device_id=(az, other), device_id_type=MESH)
+
+    def az_copy(f, step):
+        other = lax.rem(az + step, n_az)
+        return pltpu.make_async_remote_copy(
+            src_ref=packed.at[f, other], dst_ref=planes_in.at[f, az],
+            send_sem=az_send.at[f, step], recv_sem=az_recv.at[f, step],
+            device_id=(other, rad), device_id_type=MESH)
+
+    def back_copy(f, step):
+        other = lax.rem(az + step, n_az)
+        return pltpu.make_async_remote_copy(
+            src_ref=spectra.at[f, other], dst_ref=out_ref.at[f, az],
+            send_sem=back_send.at[f, step], recv_sem=back_recv.at[f, step],
+            device_id=(other, rad), device_id_type=MESH)
+
+    def own_shells(f):
+        return pltpu.make_async_copy(cells_ref.at[rad, f], shells.at[rad, f], local_sem.at[f, 0])
+
+    def own_planes(f):
+        return pltpu.make_async_copy(packed.at[f, az], planes_in.at[f, az], local_sem.at[f, 1])
+
+    def own_spectra(f):
+        return pltpu.make_async_copy(spectra.at[f, az], out_ref.at[f, az], local_sem.at[f, 2])
+
+    rad_steps = sorted(range(1, n_rad), key=lambda step: abs(step - n_rad // 2))
+    az_steps = range(1, n_az)
+
+    def start_rad(f):
+        for step in rad_steps:
+            rad_copy(f, step).start()
+        own_shells(f).start()
+
+    for f in range(min(AHEAD, fields)):
+        start_rad(f)
+
+    for f in range(fields):
+        for step in rad_steps:
+            rad_copy(f, step).wait_recv()
+        own_shells(f).wait()
+        if f + AHEAD < fields:
+            start_rad(f + AHEAD)
+
+        @pl.loop(0, slab // 4)
+        def _(part):
+            here = pl.ds(part * 4, 4)
+            rows = [shells[j, f, here].reshape(4 * planes, slots) for j in range(n_rad)]
+            dense = jnp.dot(jnp.concatenate(rows, axis=1), pack_ref[...], preferred_element_type=jnp.float32)
+            dense = dense.astype(jnp.bfloat16)
+            for k in range(n_az):
+                packed[f, k, here] = dense[:, k * block:(k + 1) * block].reshape(4, planes, block)
+
+        for step in az_steps:
+            az_copy(f, step).start()
+        own_planes(f).start()
+        for step in az_steps:
+            az_copy(f, step).wait_recv()
+        own_planes(f).wait()
+
+        @pl.loop(0, slab // 2)
+        def _(part):
+            both = [planes_in[f, :, part * 2 + x].reshape(n_az * planes, block) for x in range(2)]
+            modes = jnp.dot(cas_ref[...], jnp.concatenate(both, axis=1), preferred_element_type=jnp.float32)
+            modes = modes.astype(jnp.bfloat16)
+            for x in range(2):
+                for k in range(n_az):
+                    spectra[f, k, part * 2 + x] = modes[k * planes:(k + 1) * planes, x * block:(x + 1) * block]
+
+        for step in az_steps:
+            back_copy(f, step).start()
+        own_spectra(f).start()
+
+    for f in range(fields):
+        for step in az_steps:
+            back_copy(f, step).wait_recv()
+        own_spectra(f).wait()
+        for step in rad_steps:
+            rad_copy(f, step).wait_send()
+        for step in az_steps:
+            az_copy(f, step).wait_send()
+            back_copy(f, step).wait_send()
+
+
+def exchange(cells, pack, cas_table, n_az, n_rad):
+    _, fields, slab, planes, slots = cells.shape
+    radial = pack.shape[1]
+    block = radial // n_az
+    kind = cells.dtype
+    dma = pltpu.SemaphoreType.DMA
+    return pl.pallas_call(
+        functools.partial(exchange_kernel, n_az, n_rad),
+        in_specs=[
+            pl.BlockSpec(memory_space=pl.ANY),
+            pl.BlockSpec(memory_space=pltpu.VMEM),
+            pl.BlockSpec(memory_space=pltpu.VMEM),
+        ],
+        out_specs=pl.BlockSpec(memory_space=pl.ANY),
+        out_shape=jax.ShapeDtypeStruct((fields, n_az, slab, planes, block), kind),
+        scratch_shapes=[
+            pltpu.VMEM((n_rad, fields, slab, planes, slots), kind),
+            pltpu.VMEM((fields, n_az, slab, planes, block), kind),
+            pltpu.VMEM((fields, n_az, slab, planes, block), kind),
+            pltpu.VMEM((fields, n_az, slab, planes, block), kind),
+            dma((fields, n_rad)), dma((fields, n_rad)),
+            dma((fields, n_az)), dma((fields, n_az)),
+            dma((fields, n_az)), dma((fields, n_az)),
+            dma((fields, 3)),
+        ],
+        compiler_params=pltpu.CompilerParams(
+            collective_id=0, has_side_effects=True, vmem_limit_bytes=VMEM_LIMIT),
+    )(cells, pack, cas_table)
+
+
+def radial_kernel(modes_ref, ops_ref, which_ref, out_ref):
+    _, blocks, slab, comps, block = modes_ref.shape
+    radial = blocks * block
+    rows = [modes_ref[0, b].reshape(slab * comps, block) for b in range(blocks)]
+    rows = jnp.concatenate(rows, axis=1)
+    mapped = []
+    for n in range(2):
+        whole = lax.dot_general(rows, ops_ref[n], (((1,), (1,)), ((), ())), preferred_element_type=jnp.float32)
+        mapped.append(jnp.swapaxes(whole.reshape(slab, comps, radial), 0, 1))
+    out_ref[:, 0] = jnp.where(which_ref[...] > 0, mapped[1], mapped[0]).astype(out_ref.dtype)
+
+
+def apply_radial(modes, radial_ops, chosen_ids):
+    fields, blocks, slab, comps, block = modes.shape
+    radial = blocks * block
+    part = 16
+    which = jnp.broadcast_to(chosen_ids[:, None, None], (comps, 1, radial))
+    return pl.pallas_call(
+        radial_kernel,
+        grid=(fields, comps // part),
+        in_specs=[
+            pl.BlockSpec((1, blocks, slab, part, block), lambda f, c: (f, 0, 0, c, 0)),
+            pl.BlockSpec((2, radial, radial), lambda f, c: (0, 0, 0)),
+            pl.BlockSpec((part, 1, radial), lambda f, c: (c, 0, 0)),
+        ],
+        out_specs=pl.BlockSpec((part, 1, slab, radial), lambda f, c: (c, f, 0, 0)),
+        out_shape=jax.ShapeDtypeStruct((comps, fields, slab, radial), modes.dtype),
+        compiler_params=pltpu.CompilerParams(vmem_limit_bytes=VMEM_LIMIT),
+    )(modes, radial_ops, which)
+
+
+def per_device(field, shell_counts, op_index, radial_ops):
+    planes, fields, slots, cells = field.shape
+    n_az, n_rad = lax.axis_size("az"), lax.axis_size("rad")
+    comps_all = planes * n_az
+    radial = radial_ops.shape[1]
+    row_slot = slot_index(shell_counts, slots, radial)
+    cas_table = make_table(comps_all)
+    comp_ids = lax.axis_index("az") * planes + jnp.arange(planes, dtype=jnp.int32)
+    mode_ids = jnp.minimum(comp_ids, comps_all - comp_ids)
+    chosen_ids = jnp.take(op_index, mode_ids)
+    slab = cells // n_rad
+    if slots % 128 or cells % 128 or slab % 16 or planes % 16 or radial % (128 * n_az):
+        return plain_path(field, row_slot, cas_table, chosen_ids, radial_ops)
+    pack = (jnp.arange(n_rad * slots, dtype=jnp.int32)[:, None] == row_slot[None, :]).astype(field.dtype)
+    modes = exchange(lay_out(field, n_rad), pack, cas_table, n_az, n_rad)
+    return apply_radial(modes, radial_ops, chosen_ids)
 
 
 def solution(mesh):

time: 651 us -> 252 us (0.39); the launches traced: 639 us -> 249 us
  Pallas kernels: 0 us -> 235 us
  local copies, waits for them, and re-layouts: 223 us -> 5.8 us
  blocking collectives: 201 us -> 0 us
  waiting for transfers between devices: 165 us -> 0 us
  matrix products: 30.6 us -> 0 us
    pallas_call x0 -> x3, Pallas kernels: none -> 235 us  [the longest x1 210 us: exchange(): pl.pallas_call(functools.partial(exchange_kernel, n_az, n_rad), in_specs=...]
    all_to_all x2 -> x0, blocking collectives: 201 us -> none  [the longest x1 102 us: to_planes(): return lax.all_to_all(values, 'az', split_axis=3, concat_axis=0, tiled=True)]
    all_to_all x1 -> x0, waiting for transfers between devices: 165 us -> none  [regroup_shells(): lax.all_to_all(values, 'rad', split_axis=3, concat_axis=2, tiled=True)]
    all_to_all x6 -> x0, local copies, waits for them, and re-layouts: 103 us -> none  [the longest x2 45.6 us: to_planes(): return lax.all_to_all(values, 'az', split_axis=3, concat_axis=0, tiled=True)]
    reshape x2 -> x0, local copies, waits for them, and re-layouts: 41.3 us -> none  [the longest x1 24.4 us: transform(): values.reshape(shape[0], -1)]
    gather x3 -> x1, local copies, waits for them, and re-layouts: 39.2 us -> 0.79 us  [per_device(): chosen_ids = jnp.take(op_index, mode_ids)]
    dot_general x2 -> x0, matrix products: 30.6 us -> none  [the longest x1 19 us: per_device(): jnp.einsum('crs,cfsx->cfxr', chosen, packed, preferred_element_type=jnp.f...]
    select_n x1 -> x0, local copies, waits for them, and re-layouts: 12 us -> none  [per_device(): packed = jnp.take(slab_data, row_slot, axis=2)]
  transfers between devices with their start and end apart: 1 -> 0, of which waited for: 1 -> 0; matrix products, arithmetic and copies ran while one was open for 3% -> 0% of each run, Pallas kernels for 0% -> 0%
where the time goes in v1:
time: 252 us; the launch traced here: 249 us
  Pallas kernels  235 us (93%)
  other arithmetic  8.12 us (3%)
  local copies, waits for them, and re-layouts  5.8 us (2%)
    pallas_call x1, Pallas kernels, exchange(): pl.pallas_call(functools.partial(exchange_kernel, n_az, n_rad), in_specs=...  210 us
    pallas_call x1, Pallas kernels, lay_out(): pl.pallas_call(lay_out_kernel, grid=(fields, planes // block), in_specs=[...  14.1 us
    pallas_call x1, Pallas kernels, apply_radial(): pl.pallas_call(radial_kernel, grid=(fields, comps // part), in_specs=[pl....  11.3 us

profile of v1, /device:TPU:0, one launch (start us, length us, event | category | flops | bytes accessed | tf_op | source)
XLA Modules:
  0.0 249.5 jit_solution(8607326428548466226)
XLA Ops:
  0.0 0.0 copy-start
  0.0 0.8 reduce-window.9
  0.8 0.7 bitcast_subtract_fusion
  1.5 0.7 fusion.9
  2.2 0.1 convert_reduce_fusion
  2.3 4.3 %compare_select_fusion.1 = s32[512,1]{0,1:T(1,128)S(1)} fusion(s32[]{:T(128)} %bitcast.5, s32[]{:T(128)} %bitcast.6, s32[]{:T(128)} %bitcast.7, s32[]{:T(128)} %bitcast.8, s32[]{:T(128)} %bitcast.9, s32[]{:T(128)} %bitcast.11, s32[]{:T(128)} %bitcast.10, s32[512,1]{0,1:T(1,128)S(1)} %bitcast.18, s32[512,1]{0,1:T(1,128)S(1)} %bitcast.16), kind=kLoop, calls=%fused_computation.17 | loop fusion | flops 7168 | bytes 6172 | tf_op jit(solution)/shard_map/jit(_take)/gather | solution.py:27
  6.6 0.7 fusion.7
  7.3 0.4 fusion.pack_ref
  7.7 14.1 %shard_map.46.cells_ref = bf16[8,4,16,64,128]{4,3,2,1,0:T(8,128)(2,1)} custom-call(bf16[64,4,128,128]{3,2,1,0:T(8,128)(2,1)} %field_ref.1), custom_call_target="tpu_custom_call" | custom-call | tf_op jit(solution)/shard_map/pallas_call | solution.py:70
  21.8 1.1 multiply_convert_fusion.cas_ref
  22.9 0.0 copy-start.3
  22.9 210.0 %shard_map.47.modes_ref = bf16[4,4,16,64,128]{4,3,2,1,0:T(8,128)(2,1)S(1)} custom-call(bf16[8,4,16,64,128]{4,3,2,1,0:T(8,128)(2,1)} %shard_map.46.cells_ref, bf16[1024,512]{1,0:T(8,128)(2,1)S(1)} %fusion.pack_ref, bf16[256,256]{1,0:T(8,128)(2,1)S(1)} %multiply_convert_fusion.cas_ref), custom_call_target="tpu_custom_call" | custom-call | tf_op jit(solution)/shard_map/pallas_call | solution.py:187
  233.0 0.0 copy-start.1
  233.0 2.0 copy-done.1
  235.0 0.0 copy-done
  235.0 0.8 gather_fusion
  235.8 0.1 broadcast_in_dim.16.which_ref
  236.0 0.0 copy-done.3
  236.0 0.0 copy-start.2
  236.0 2.2 copy-done.2
  238.2 11.3 %shard_map.48 = bf16[64,4,16,512]{3,2,1,0:T(8,128)(2,1)} custom-call(bf16[4,4,16,64,128]{4,3,2,1,0:T(8,128)(2,1)S(1)} %copy-done.2, bf16[2,512,512]{2,1,0:T(8,128)(2,1)S(1)} %copy-done.3, s32[64,1,512]{2,1,0:T(1,128)S(1)} %broadcast_in_dim.16.which_ref), custom_call_target="tpu_custom_call" | custom-call | tf_op jit(solution)/shard_map/pallas_call | solution.py:228
  (5 shorter events, 0.1 us)
Async XLA Ops:
  0.0 235.0 %copy-start = (s32[129]{0:T(256)S(1)}, s32[129]{0:T(256)}, u32[]{:S(2)}) copy-start(s32[129]{0:T(256)} %param.6) | copy-start | bytes 1552
  22.9 213.1 %copy-start.3 = (bf16[2,512,512]{2,1,0:T(8,128)(2,1)S(1)}, bf16[2,512,512]{2,1,0:T(8,128)(2,1)}, u32[]{:S(2)}) copy-start(bf16[2,512,512]{2,1,0:T(8,128)(2,1)} %ops_ref.1) | copy-start | bytes 3145732
  233.0 2.0 copy-start.1
  236.0 2.2 copy-start.2

commit v2 on v1

v2 whole, which is shorter than its diff:
```python
import functools
import math

import jax
import jax.numpy as jnp
from jax import lax
from jax.experimental import pallas as pl
from jax.experimental.pallas import tpu as pltpu
from jax.sharding import PartitionSpec as P

MESH = pl.DeviceIdType.MESH
VMEM_LIMIT = 56 << 20
PART = 4


def make_table(length):
    index = jnp.arange(length, dtype=jnp.int32)
    product = index[:, None] * index[None, :] % length
    angle = product.astype(jnp.float32) * (2.0 * math.pi / length)
    return ((jnp.cos(angle) + jnp.sin(angle)) * (1.0 / math.sqrt(length))).astype(jnp.bfloat16)


def slot_index(counts, capacity, radial):
    starts = jnp.cumsum(counts) - counts
    rows = jnp.arange(radial, dtype=jnp.int32)
    owner = jnp.sum((starts[None, :] <= rows[:, None]).astype(jnp.int32), axis=1) - 1
    return owner * capacity + rows - jnp.take(starts, owner)


def to_planes(values):
    return lax.all_to_all(values, "az", split_axis=3, concat_axis=0, tiled=True)


def to_modes(values):
    return lax.all_to_all(values, "az", split_axis=0, concat_axis=3, tiled=True)


def regroup_shells(values):
    return lax.all_to_all(values, "rad", split_axis=3, concat_axis=2, tiled=True)


def transform(cas_table, values):
    shape = values.shape
    flat = jnp.dot(cas_table, values.reshape(shape[0], -1), preferred_element_type=jnp.float32)
    return flat.astype(jnp.bfloat16).reshape(shape)


def plain_path(field, row_slot, cas_table, chosen_ids, radial_ops):
    chosen = jnp.take(radial_ops, chosen_ids, axis=0)
    gathered = to_planes(field)
    spectra = transform(cas_table, gathered)
    returned = to_modes(spectra)
    slab_data = regroup_shells(returned)
    packed = jnp.take(slab_data, row_slot, axis=2)
    result = jnp.einsum("crs,cfsx->cfxr", chosen, packed, preferred_element_type=jnp.float32)
    return result.astype(jnp.bfloat16)


def exchange_kernel(n_az, n_rad, field_ref, pack_ref, cas_ref, out_ref, raw, cells, shells, packed,
                    planes_in, spectra, rad_send, rad_recv, az_send, az_recv, back_send, back_recv,
                    own_sem, raw_sem):
    az, rad = lax.axis_index("az"), lax.axis_index("rad")
    _, fields, slab, planes, slots = shells.shape
    block = packed.shape[4]
    parts = slab // PART
    chunks = fields * parts

    def raw_copy(f):
        return pltpu.make_async_copy(field_ref.at[:, f], raw.at[f], raw_sem.at[f])

    for f in range(fields):
        raw_copy(f).start()

    barrier = pltpu.get_barrier_semaphore()
    for step in range(1, n_rad):
        pl.semaphore_signal(barrier, inc=1, device_id=(az, lax.rem(rad + step, n_rad)), device_id_type=MESH)
    for step in range(1, n_az):
        pl.semaphore_signal(barrier, inc=1, device_id=(lax.rem(az + step, n_az), rad), device_id_type=MESH)

    def place(q):
        return q // parts, pl.ds((q % parts) * PART, PART)

    def rad_copy(q, step):
        f, here = place(q)
        other = lax.rem(rad + step, n_rad)
        return pltpu.make_async_remote_copy(
            src_ref=cells.at[other, f, here], dst_ref=shells.at[rad, f, here],
            send_sem=rad_send.at[q, step], recv_sem=rad_recv.at[q, step],
            device_id=(az, other), device_id_type=MESH)

    def az_copy(q, step):
        f, here = place(q)
        other = lax.rem(az + step, n_az)
        return pltpu.make_async_remote_copy(
            src_ref=packed.at[f, other, here], dst_ref=planes_in.at[f, az, here],
            send_sem=az_send.at[q, step], recv_sem=az_recv.at[q, step],
            device_id=(other, rad), device_id_type=MESH)

    def back_copy(q, step):
        f, here = place(q)
        other = lax.rem(az + step, n_az)
        return pltpu.make_async_remote_copy(
            src_ref=spectra.at[f, other, here], dst_ref=out_ref.at[f, az, here],
            send_sem=back_send.at[q, step], recv_sem=back_recv.at[q, step],
            device_id=(other, rad), device_id_type=MESH)

    def own_shells(q):
        f, here = place(q)
        return pltpu.make_async_copy(cells.at[rad, f, here], shells.at[rad, f, here], own_sem.at[q, 0])

    def own_planes(q):
        f, here = place(q)
        return pltpu.make_async_copy(packed.at[f, az, here], planes_in.at[f, az, here], own_sem.at[q, 1])

    def own_spectra(q):
        f, here = place(q)
        return pltpu.make_async_copy(spectra.at[f, az, here], out_ref.at[f, az, here], own_sem.at[q, 2])

    rad_steps = sorted(range(1, n_rad), key=lambda step: abs(step - n_rad // 2))
    az_steps = range(1, n_az)

    def lay_out(f):
        raw_copy(f).wait()

        @pl.loop(0, planes // 16)
        def _(part):
            here = pl.ds(part * 16, 16)
            turned = jnp.swapaxes(raw[f, here], 1, 2)
            by_cell = jnp.swapaxes(turned, 0, 1)
            cells[:, f, :, here, :] = by_cell.reshape(n_rad, slab, 16, slots)

    def start_rad(q):
        for step in rad_steps:
            rad_copy(q, step).start()
        own_shells(q).start()

    def finish(q):
        f, _ = place(q)
        for step in az_steps:
            az_copy(q, step).wait_recv()
        own_planes(q).wait()

        @pl.loop(0, PART // 2)
        def _(pair):
            first = (q % parts) * PART + pair * 2
            both = [planes_in[f, :, first + x].reshape(n_az * planes, block) for x in range(2)]
            modes = jnp.dot(cas_ref[...], jnp.concatenate(both, axis=1), preferred_element_type=jnp.float32)
            modes = modes.astype(jnp.bfloat16)
            for x in range(2):
                for k in range(n_az):
                    spectra[f, k, first + x] = modes[k * planes:(k + 1) * planes, x * block:(x + 1) * block]

        for step in az_steps:
            back_copy(q, step).start()
        own_spectra(q).start()

    lay_out(0)
    pl.semaphore_wait(barrier, n_rad + n_az - 2)
    for q in range(parts):
        start_rad(q)

    @pl.loop(0, chunks)
    def _(q):
        f, here = place(q)

        @pl.when((q % parts == 0) & (f + 1 < fields))
        def _():
            lay_out(f + 1)

        for step in rad_steps:
            rad_copy(q, step).wait_recv()
        own_shells(q).wait()

        @pl.when(q + parts < chunks)
        def _():
            start_rad(q + parts)

        rows = [shells[j, f, here].reshape(PART * planes, slots) for j in range(n_rad)]
        dense = jnp.dot(jnp.concatenate(rows, axis=1), pack_ref[...], preferred_element_type=jnp.float32)
        dense = dense.astype(jnp.bfloat16)
        for k in range(n_az):
            packed[f, k, here] = dense[:, k * block:(k + 1) * block].reshape(PART, planes, block)

        for step in az_steps:
            az_copy(q, step).start()
        own_planes(q).start()

        @pl.when(q > 0)
        def _():
            finish(q - 1)

    finish(chunks - 1)

    @pl.loop(0, chunks)
    def _(q):
        for step in az_steps:
            back_copy(q, step).wait_recv()
        own_spectra(q).wait()
        for step in rad_steps:
            rad_copy(q, step).wait_send()
        for step in az_steps:
            az_copy(q, step).wait_send()
            back_copy(q, step).wait_send()


def exchange(field, pack, cas_table, n_az, n_rad):
    planes, fields, slots, length = field.shape
    slab = length // n_rad
    block = pack.shape[1] // n_az
    chunks = fields * slab // PART
    kind = field.dtype
    dma = pltpu.SemaphoreType.DMA
    return pl.pallas_call(
        functools.partial(exchange_kernel, n_az, n_rad),
        in_specs=[
            pl.BlockSpec(memory_space=pl.ANY),
            pl.BlockSpec(memory_space=pltpu.VMEM),
            pl.BlockSpec(memory_space=pltpu.VMEM),
        ],
        out_specs=pl.BlockSpec(memory_space=pl.ANY),
        out_shape=jax.ShapeDtypeStruct((fields, n_az, slab, planes, block), kind),
        scratch_shapes=[
            pltpu.VMEM((fields, planes, slots, length), kind),
            pltpu.VMEM((n_rad, fields, slab, planes, slots), kind),
            pltpu.VMEM((n_rad, fields, slab, planes, slots), kind),
            pltpu.VMEM((fields, n_az, slab, planes, block), kind),
            pltpu.VMEM((fields, n_az, slab, planes, block), kind),
            pltpu.VMEM((fields, n_az, slab, planes, block), kind),
            dma((chunks, n_rad)), dma((chunks, n_rad)),
            dma((chunks, n_az)), dma((chunks, n_az)),
            dma((chunks, n_az)), dma((chunks, n_az)),
            dma((chunks, 3)), dma((fields,)),
        ],
        compiler_params=pltpu.CompilerParams(
            collective_id=0, has_side_effects=True, vmem_limit_bytes=VMEM_LIMIT),
    )(field, pack, cas_table)


def radial_kernel(modes_ref, ops_ref, which_ref, out_ref):
    _, blocks, slab, comps, block = modes_ref.shape
    radial = blocks * block
    rows = [modes_ref[0, b].reshape(slab * comps, block) for b in range(blocks)]
    rows = jnp.concatenate(rows, axis=1)
    mapped = []
    for n in range(2):
        whole = lax.dot_general(rows, ops_ref[n], (((1,), (1,)), ((), ())), preferred_element_type=jnp.float32)
        mapped.append(whole.reshape(slab, comps, radial))
    picked = jnp.where(which_ref[...] > 0, mapped[1], mapped[0])
    out_ref[:, 0] = jnp.swapaxes(picked, 0, 1).astype(out_ref.dtype)


def apply_radial(modes, radial_ops, chosen_ids):
    fields, blocks, slab, comps, block = modes.shape
    radial = blocks * block
    part = 16
    which = jnp.broadcast_to(chosen_ids[None, :, None], (1, comps, radial))
    return pl.pallas_call(
        radial_kernel,
        grid=(fields, comps // part),
        in_specs=[
            pl.BlockSpec((1, blocks, slab, part, block), lambda f, c: (f, 0, 0, c, 0)),
            pl.BlockSpec((2, radial, radial), lambda f, c: (0, 0, 0)),
            pl.BlockSpec((1, part, radial), lambda f, c: (0, c, 0)),
        ],
        out_specs=pl.BlockSpec((part, 1, slab, radial), lambda f, c: (c, f, 0, 0)),
        out_shape=jax.ShapeDtypeStruct((comps, fields, slab, radial), modes.dtype),
        compiler_params=pltpu.CompilerParams(vmem_limit_bytes=VMEM_LIMIT),
    )(modes, radial_ops, which)


def per_device(field, shell_counts, op_index, radial_ops):
    planes, fields, slots, cells = field.shape
    n_az, n_rad = lax.axis_size("az"), lax.axis_size("rad")
    comps_all = planes * n_az
    radial = radial_ops.shape[1]
    cas_table = make_table(comps_all)
    comp_ids = lax.axis_index("az") * planes + jnp.arange(planes, dtype=jnp.int32)
    mode_ids = jnp.minimum(comp_ids, comps_all - comp_ids)
    slab = cells // n_rad
    if slots % 128 or cells % 128 or slab % 16 or planes % 16 or radial % (128 * n_az):
        row_slot = slot_index(shell_counts, slots, radial)
        return plain_path(field, row_slot, cas_table, jnp.take(op_index, mode_ids), radial_ops)
    shells = jnp.arange(n_rad, dtype=jnp.int32)
    starts = jnp.sum(jnp.where(shells[None, :] < shells[:, None], shell_counts[None, :], 0), axis=1)
    slot = jnp.arange(slots, dtype=jnp.int32)[None, :]
    row_of = jnp.where(slot < shell_counts[:, None], starts[:, None] + slot, -1)
    pack = row_of[:, :, None] == jnp.arange(radial, dtype=jnp.int32)[None, None, :]
    pack = pack.astype(field.dtype).reshape(n_rad * slots, radial)
    numbers = jnp.arange(op_index.shape[0], dtype=jnp.int32)
    chosen_ids = jnp.sum(jnp.where(mode_ids[:, None] == numbers[None, :], op_index[None, :], 0), axis=1)
    modes = exchange(field, pack, cas_table, n_az, n_rad)
    return apply_radial(modes, radial_ops, chosen_ids)


def solution(mesh):
    return jax.shard_map(
        per_device,
        mesh=mesh,
        in_specs=(P("az", None, "rad", None), P(), P(), P()),
        out_specs=P("az", None, "rad", None),
        check_vma=False,
    )
```

time: 252 us -> 224 us (0.89)
  Pallas kernels: 235 us -> 216 us
  local copies, waits for them, and re-layouts: 5.8 us -> 0.72 us
  other arithmetic: 8.12 us -> 5.28 us
    pallas_call x1 -> x0, Pallas kernels: 14.1 us -> none  [lay_out(): pl.pallas_call(lay_out_kernel, grid=(fields, planes // block), in_specs=[...]
    pallas_call x1, Pallas kernels: 210 us -> 202 us  [exchange(): pl.pallas_call(functools.partial(exchange_kernel, n_az, n_rad), in_specs=...]
    gather x3 -> x0, other arithmetic: 4.34 us -> none  [the longest x2 4.33 us: slot_index(): return owner * capacity + rows - jnp.take(starts, owner)]
    unnamed x8 -> x0, local copies, waits for them, and re-layouts: 4.2 us -> none
    pallas_call x1, Pallas kernels: 11.3 us -> 14.6 us  [apply_radial(): pl.pallas_call(radial_kernel, grid=(fields, comps // part), in_specs=[pl....]
where the time goes in v2:
time: 224 us; the launch traced here: 222 us
  Pallas kernels  216 us (96%)
  other arithmetic  5.28 us (2%)
    pallas_call x1, Pallas kernels, exchange(): pl.pallas_call(functools.partial(exchange_kernel, n_az, n_rad), in_specs=...  202 us
    pallas_call x1, Pallas kernels, apply_radial(): pl.pallas_call(radial_kernel, grid=(fields, comps // part), in_specs=[pl....  14.6 us

profile of v2, /device:TPU:0, one launch (start us, length us, event | category | flops | bytes accessed | tf_op | source)
XLA Modules:
  0.0 222.4 jit_solution(10628228110405170510)
XLA Ops:
  0.0 0.9 select_reduce_fusion
  0.9 0.8 select_reduce_fusion.1
  1.6 0.7 select_bitcast_fusion
  2.4 0.7 broadcast_in_dim.52.which_ref
  3.1 1.7 multiply_convert_fusion.cas_ref
  4.8 1.2 fusion.pack_ref
  6.0 201.8 %shard_map.46.modes_ref = bf16[4,4,16,64,128]{4,3,2,1,0:T(8,128)(2,1)} custom-call(bf16[64,4,128,128]{3,2,1,0:T(8,128)(2,1)} %field_ref.1, bf16[1024,512]{1,0:T(8,128)(2,1)} %fusion.pack_ref, bf16[256,256]{1,0:T(8,128)(2,1)} %multiply_convert_fusion.cas_ref), custom_call_target="tpu_custom_call" | custom-call | tf_op jit(solution)/shard_map/pallas_call | solution.py:213
  207.8 14.6 %shard_map.47 = bf16[64,4,16,512]{3,2,1,0:T(8,128)(2,1)} custom-call(bf16[4,4,16,64,128]{4,3,2,1,0:T(8,128)(2,1)} %shard_map.46.modes_ref, bf16[2,512,512]{2,1,0:T(8,128)(2,1)} %ops_ref.1, s32[1,64,512]{2,1,0:T(8,128)} %broadcast_in_dim.52.which_ref), custom_call_target="tpu_custom_call" | custom-call | tf_op jit(solution)/shard_map/pallas_call | solution.py:257
  (1 shorter events, 0.0 us)

commit v3 on v2

--- a/solution.py
+++ b/solution.py
@@ -11,6 +11,7 @@
 MESH = pl.DeviceIdType.MESH
 VMEM_LIMIT = 56 << 20
 PART = 4
+AHEAD = 3
 
 
 def make_table(length):
@@ -236,6 +237,250 @@
     )(field, pack, cas_table)
 
 
+def chip_kernel(n_az, n_rad, field_ref, near_ref, rest_ref, first_ref, second_ref, cas_ref, out_ref,
+                raw, cells, beside, outgoing, shells, packed, planes_in, spectra, pair_send, pair_recv,
+                rad_send, rad_recv, az_send, az_recv, back_send, back_recv, own_sem, raw_sem):
+    az, rad = lax.axis_index("az"), lax.axis_index("rad")
+    chip, core = rad // 2, rad % 2
+    _, fields, slab, planes, slots = cells.shape
+    block = packed.shape[4]
+    half = planes // 2
+    parts = slab // PART
+    chunks = fields * parts
+
+    def raw_copy(f):
+        return pltpu.make_async_copy(field_ref.at[:, f], raw.at[f], raw_sem.at[f])
+
+    for f in range(fields):
+        raw_copy(f).start()
+
+    barrier = pltpu.get_barrier_semaphore()
+    for step in range(1, n_rad):
+        pl.semaphore_signal(barrier, inc=1, device_id=(az, lax.rem(rad + step, n_rad)), device_id_type=MESH)
+    for step in range(1, n_az):
+        pl.semaphore_signal(barrier, inc=1, device_id=(lax.rem(az + step, n_az), rad), device_id_type=MESH)
+
+    def place(q):
+        return q // parts, pl.ds((q % parts) * PART, PART)
+
+    def halves(which):
+        return pl.ds(pl.multiple_of(which * half, half), half)
+
+    def pair_copy(q):
+        f, here = place(q)
+        return pltpu.make_async_remote_copy(
+            src_ref=cells.at[:, f, here, halves(1 - core)], dst_ref=beside.at[q],
+            send_sem=pair_send.at[q], recv_sem=pair_recv.at[q],
+            device_id=(az, chip * 2 + 1 - core), device_id_type=MESH)
+
+    def rad_copy(q, step):
+        other = lax.rem(rad + step, n_rad)
+        return pltpu.make_async_remote_copy(
+            src_ref=outgoing.at[other, q], dst_ref=shells.at[chip, q, :, halves(core)],
+            send_sem=rad_send.at[q, step], recv_sem=rad_recv.at[q, step],
+            device_id=(az, other), device_id_type=MESH)
+
+    def az_copy(q, step):
+        f, here = place(q)
+        other = lax.rem(az + step, n_az)
+        return pltpu.make_async_remote_copy(
+            src_ref=packed.at[f, other, here], dst_ref=planes_in.at[f, az, here],
+            send_sem=az_send.at[q, step], recv_sem=az_recv.at[q, step],
+            device_id=(other, rad), device_id_type=MESH)
+
+    def back_copy(q, step):
+        f, here = place(q)
+        other = lax.rem(az + step, n_az)
+        return pltpu.make_async_remote_copy(
+            src_ref=spectra.at[f, other, here], dst_ref=out_ref.at[f, az, here],
+            send_sem=back_send.at[q, step], recv_sem=back_recv.at[q, step],
+            device_id=(other, rad), device_id_type=MESH)
+
+    def own_shells(q):
+        return pltpu.make_async_copy(
+            outgoing.at[rad, q], shells.at[chip, q, :, halves(core)], own_sem.at[q, 0])
+
+    def own_planes(q):
+        f, here = place(q)
+        return pltpu.make_async_copy(packed.at[f, az, here], planes_in.at[f, az, here], own_sem.at[q, 1])
+
+    def own_spectra(q):
+        f, here = place(q)
+        return pltpu.make_async_copy(spectra.at[f, az, here], out_ref.at[f, az, here], own_sem.at[q, 2])
+
+    rad_steps = sorted(range(1, n_rad), key=lambda step: abs(step - n_rad // 2))
+    az_steps = range(1, n_az)
+
+    def lay_out(f):
+        raw_copy(f).wait()
+
+        @pl.loop(0, planes // 16)
+        def _(part):
+            here = pl.ds(part * 16, 16)
+            turned = jnp.swapaxes(raw[f, here], 1, 2)
+            by_cell = jnp.swapaxes(turned, 0, 1)
+            cells[:, f, :, here, :] = by_cell.reshape(n_rad, slab, 16, slots)
+
+    def start_rad(q):
+        f, here = place(q)
+        pair_copy(q).wait_recv()
+
+        @pl.loop(0, n_rad // 4)
+        def _(group):
+            to = pl.ds(group * 4, 4)
+            mine = cells[to, f, here, halves(core)].reshape(4 * PART * half, slots)
+            both = jnp.concatenate([mine, beside[q, to].reshape(4 * PART * half, slots)], axis=1)
+            near = jnp.dot(both, near_ref[...], preferred_element_type=jnp.float32)
+            outgoing[to, q, :PART] = near.astype(jnp.bfloat16).reshape(4, PART, half, slots)
+            split = both.reshape(4, PART, half, 2 * slots)
+            ends = [split[:, :PART // 2], split[:, PART // 2:]]
+            ends = [end.reshape(4 * PART // 2 * half, 2 * slots) for end in ends]
+            rest = jnp.dot(jnp.concatenate(ends, axis=1), rest_ref[...], preferred_element_type=jnp.float32)
+            outgoing[to, q, PART:] = rest.astype(jnp.bfloat16).reshape(4, PART // 2, half, slots)
+
+        for step in rad_steps:
+            rad_copy(q, step).start()
+        own_shells(q).start()
+
+    def finish(q):
+        f, _ = place(q)
+        for step in az_steps:
+            az_copy(q, step).wait_recv()
+        own_planes(q).wait()
+
+        @pl.loop(0, PART // 2)
+        def _(pair):
+            first = (q % parts) * PART + pair * 2
+            both = [planes_in[f, :, first + x].reshape(n_az * planes, block) for x in range(2)]
+            modes = jnp.dot(cas_ref[...], jnp.concatenate(both, axis=1), preferred_element_type=jnp.float32)
+            modes = modes.astype(jnp.bfloat16)
+            for x in range(2):
+                for k in range(n_az):
+                    spectra[f, k, first + x] = modes[k * planes:(k + 1) * planes, x * block:(x + 1) * block]
+
+        for step in az_steps:
+            back_copy(q, step).start()
+        own_spectra(q).start()
+
+    lay_out(0)
+    pl.semaphore_wait(barrier, n_rad + n_az - 2)
+    for q in range(parts):
+        pair_copy(q).start()
+
+    @pl.loop(0, AHEAD)
+    def _(q):
+        start_rad(q)
+
+    @pl.loop(0, chunks)
+    def _(q):
+        f, here = place(q)
+
+        @pl.when((q % parts == 0) & (f + 1 < fields))
+        def _():
+            lay_out(f + 1)
+            for part in range(parts):
+                pair_copy(q + parts + part).start()
+
+        @pl.when(q + AHEAD < chunks)
+        def _():
+            start_rad(q + AHEAD)
+
+        for step in rad_steps:
+            rad_copy(q, step).wait_recv()
+        own_shells(q).wait()
+
+        chips = range(n_rad // 2)
+        rows = [shells[j, q, :PART].reshape(PART * planes, slots) for j in chips]
+        dense = jnp.dot(jnp.concatenate(rows, axis=1), first_ref[...], preferred_element_type=jnp.float32)
+        rows = [shells[j, q, PART:].reshape(PART // 2 * planes, slots) for j in chips]
+        rows = jnp.concatenate(rows, axis=1)
+        rest = [jnp.dot(rows, second_ref[n], preferred_element_type=jnp.float32) for n in range(2)]
+        dense = dense + jnp.concatenate(rest, axis=0)
+        dense = dense.astype(jnp.bfloat16)
+        for k in range(n_az):
+            packed[f, k, here] = dense[:, k * block:(k + 1) * block].reshape(PART, planes, block)
+
+        for step in az_steps:
+            az_copy(q, step).start()
+        own_planes(q).start()
+
+        @pl.when(q > 0)
+        def _():
+            finish(q - 1)
+
+    finish(chunks - 1)
+
+    @pl.loop(0, chunks)
+    def _(q):
+        for step in az_steps:
+            back_copy(q, step).wait_recv()
+        own_spectra(q).wait()
+        pair_copy(q).wait_send()
+        for step in rad_steps:
+            rad_copy(q, step).wait_send()
+        for step in az_steps:
+            az_copy(q, step).wait_send()
+            back_copy(q, step).wait_send()
+
+
+def exchange_packed(field, shell_counts, starts, radial, cas_table, n_az, n_rad):
+    planes, fields, slots, length = field.shape
+    slab = length // n_rad
+    block = radial // n_az
+    chunks = fields * slab // PART
+    units = PART + PART // 2
+    kind = field.dtype
+    dma = pltpu.SemaphoreType.DMA
+    rad = lax.axis_index("rad")
+    index = jnp.arange(n_rad, dtype=jnp.int32)
+    count_of = lambda which: jnp.sum(jnp.where(index == which, shell_counts, 0))
+    slot = jnp.arange(slots, dtype=jnp.int32)
+    other = rad + 1 - 2 * (rad % 2)
+    mine, theirs = count_of(rad), count_of(other)
+    spot = jnp.concatenate([
+        jnp.where(slot < mine, slot + jnp.where(rad % 2 == 1, theirs, 0), -1),
+        jnp.where(slot < theirs, slot + jnp.where(rad % 2 == 1, 0, mine), -1)])
+    near = (spot[:, None] == slot[None, :]).astype(kind)
+    late = jnp.where((slot < slots // 2)[None, :], spot[:, None] == slots + slot[None, :], False)
+    later = jnp.where((slot >= slots // 2)[None, :], spot[:, None] == slots // 2 + slot[None, :], False)
+    rest = jnp.concatenate([late, later], axis=0).astype(kind)
+    totals = shell_counts[0::2] + shell_counts[1::2]
+    begins = starts[0::2]
+    rows = jnp.arange(radial, dtype=jnp.int32)[None, None, :]
+
+    def rows_of(places):
+        row = jnp.where((places[None, :] >= 0) & (places[None, :] < totals[:, None]), begins[:, None] + places[None, :], -1)
+        return (row[:, :, None] == rows).astype(kind).reshape(-1, radial)
+
+    first = rows_of(slot)
+    second = jnp.stack([
+        rows_of(jnp.where(slot < slots // 2, slots + slot, -1)),
+        rows_of(jnp.where(slot >= slots // 2, slots // 2 + slot, -1))])
+    return pl.pallas_call(
+        functools.partial(chip_kernel, n_az, n_rad),
+        in_specs=[pl.BlockSpec(memory_space=pl.ANY)] + [pl.BlockSpec(memory_space=pltpu.VMEM)] * 5,
+        out_specs=pl.BlockSpec(memory_space=pl.ANY),
+        out_shape=jax.ShapeDtypeStruct((fields, n_az, slab, planes, block), kind),
+        scratch_shapes=[
+            pltpu.VMEM((fields, planes, slots, length), kind),
+            pltpu.VMEM((n_rad, fields, slab, planes, slots), kind),
+            pltpu.VMEM((chunks, n_rad, PART, planes // 2, slots), kind),
+            pltpu.VMEM((n_rad, chunks, units, planes // 2, slots), kind),
+            pltpu.VMEM((n_rad // 2, chunks, units, planes, slots), kind),
+            pltpu.VMEM((fields, n_az, slab, planes, block), kind),
+            pltpu.VMEM((fields, n_az, slab, planes, block), kind),
+            pltpu.VMEM((fields, n_az, slab, planes, block), kind),
+            dma((chunks,)), dma((chunks,)),
+            dma((chunks, n_rad)), dma((chunks, n_rad)),
+            dma((chunks, n_az)), dma((chunks, n_az)),
+            dma((chunks, n_az)), dma((chunks, n_az)),
+            dma((chunks, 3)), dma((fields,)),
+        ],
+        compiler_params=pltpu.CompilerParams(
+            collective_id=1, has_side_effects=True, vmem_limit_bytes=VMEM_LIMIT),
+    )(field, near, rest, first, second, cas_table)
+
+
 def radial_kernel(modes_ref, ops_ref, which_ref, out_ref):
     _, blocks, slab, comps, block = modes_ref.shape
     radial = blocks * block
@@ -277,18 +522,26 @@
     comp_ids = lax.axis_index("az") * planes + jnp.arange(planes, dtype=jnp.int32)
     mode_ids = jnp.minimum(comp_ids, comps_all - comp_ids)
     slab = cells // n_rad
-    if slots % 128 or cells % 128 or slab % 16 or planes % 16 or radial % (128 * n_az):
+    if slots % 128 or cells % 128 or n_rad % 4 or slab % 16 or planes % 32 or radial % (128 * n_az):
         row_slot = slot_index(shell_counts, slots, radial)
         return plain_path(field, row_slot, cas_table, jnp.take(op_index, mode_ids), radial_ops)
     shells = jnp.arange(n_rad, dtype=jnp.int32)
     starts = jnp.sum(jnp.where(shells[None, :] < shells[:, None], shell_counts[None, :], 0), axis=1)
-    slot = jnp.arange(slots, dtype=jnp.int32)[None, :]
-    row_of = jnp.where(slot < shell_counts[:, None], starts[:, None] + slot, -1)
-    pack = row_of[:, :, None] == jnp.arange(radial, dtype=jnp.int32)[None, None, :]
-    pack = pack.astype(field.dtype).reshape(n_rad * slots, radial)
+
+    def any_counts():
+        slot = jnp.arange(slots, dtype=jnp.int32)[None, :]
+        row_of = jnp.where(slot < shell_counts[:, None], starts[:, None] + slot, -1)
+        pack = row_of[:, :, None] == jnp.arange(radial, dtype=jnp.int32)[None, None, :]
+        pack = pack.astype(field.dtype).reshape(n_rad * slots, radial)
+        return exchange(field, pack, cas_table, n_az, n_rad)
+
+    def even_counts():
+        return exchange_packed(field, shell_counts, starts, radial, cas_table, n_az, n_rad)
+
     numbers = jnp.arange(op_index.shape[0], dtype=jnp.int32)
     chosen_ids = jnp.sum(jnp.where(mode_ids[:, None] == numbers[None, :], op_index[None, :], 0), axis=1)
-    modes = exchange(field, pack, cas_table, n_az, n_rad)
+    fullest = jnp.max(shell_counts[0::2] + shell_counts[1::2])
+    modes = lax.cond(2 * fullest <= 3 * slots, even_counts, any_counts)
     return apply_radial(modes, radial_ops, chosen_ids)
 
 

time: 224 us -> 226 us (level)
  no operation moved by 1% of the time
where the time goes in v3:
time: 226 us; the launch traced here: 224 us
  Pallas kernels  216 us (96%)
  other arithmetic  4.62 us (2%)
    pallas_call x1, Pallas kernels, exchange(): pl.pallas_call(functools.partial(exchange_kernel, n_az, n_rad), in_specs=...  202 us
    pallas_call x1, Pallas kernels, apply_radial(): pl.pallas_call(radial_kernel, grid=(fields, comps // part), in_specs=[pl....  14.5 us

profile of v3, /device:TPU:0, one launch (start us, length us, event | category | flops | bytes accessed | tf_op | source)
XLA Modules:
  0.0 223.8 jit_solution(11552888908611011833)
XLA Ops:
  0.0 1.1 multiply_convert_fusion
  1.1 0.8 select_reduce_fusion.1
  1.9 0.7 slice.15
  2.6 0.7 slice.16
  3.4 0.6 add_reduce_fusion
  4.7 0.0 copy-start
  4.7 203.6 %conditional.1 = (bf16[4,4,16,64,128]{4,3,2,1,0:T(8,128)(2,1)}) conditional(s32[]{:T(128)} %convert_element_type.43, (s32[8]{0:T(128)}, s32[8]{0:T(128)S(1)}, bf16[64,4,128,128]{3,2,1,0:T(8,128)(2,1)}, bf16[256,256]{1,0:T(8,128)(2,1)S(1)}) %tuple.11, (s32[8]{0:T(128)}, s32[8]{0:T(128)S(1)}, bf16[64,4,128,128]{3,2,1,0:T(8,128)(2,1)}, ...), branch_computations={%region_2.3_spmd, %region_3.6_spmd} | conditional | flops 2433861 | bytes 2979264 | solution.py:544
  4.7 0.7 select_bitcast_fusion
  5.4 1.2 fusion.pack_ref
  6.6 201.7 %branch_0_fun.1 = bf16[4,4,16,64,128]{4,3,2,1,0:T(8,128)(2,1)} custom-call(bf16[64,4,128,128]{3,2,1,0:T(8,128)(2,1)} %get-tuple-element.24.field_ref, bf16[1024,512]{1,0:T(8,128)(2,1)} %fusion.pack_ref, bf16[256,256]{1,0:T(8,128)(2,1)S(1)} %get-tuple-element.27.cas_ref), custom_call_target="tpu_custom_call" | custom-call | tf_op jit(solution)/shard_map/cond/branch_0_fun/pallas_call | solution.py:214
  208.3 0.0 copy-done
  208.3 0.2 select_reduce_fusion
  208.5 0.7 broadcast_in_dim.75.which_ref
  209.3 14.5 %shard_map.46 = bf16[64,4,16,512]{3,2,1,0:T(8,128)(2,1)} custom-call(bf16[4,4,16,64,128]{4,3,2,1,0:T(8,128)(2,1)} %get-tuple-element.48.modes_ref, bf16[2,512,512]{2,1,0:T(8,128)(2,1)} %ops_ref.1, s32[1,64,512]{2,1,0:T(8,128)} %broadcast_in_dim.75.which_ref), custom_call_target="tpu_custom_call" | custom-call | tf_op jit(solution)/shard_map/pallas_call | solution.py:502
  (1 shorter events, 0.0 us)
Async XLA Ops:
  4.7 203.7 %copy-start = (s32[129]{0:T(256)S(1)}, s32[129]{0:T(256)}, u32[]{:S(2)}) copy-start(s32[129]{0:T(256)} %param.8) | copy-start | bytes 1552

commit v4 on v2

v4 whole, which is shorter than its diff:
```python
import functools
import math

import jax
import jax.numpy as jnp
from jax import lax
from jax.experimental import pallas as pl
from jax.experimental.pallas import tpu as pltpu
from jax.sharding import PartitionSpec as P

MESH = pl.DeviceIdType.MESH
VMEM_LIMIT = 60 << 20
PART = 4
AHEAD = 2


def make_table(length):
    index = jnp.arange(length, dtype=jnp.int32)
    product = index[:, None] * index[None, :] % length
    angle = product.astype(jnp.float32) * (2.0 * math.pi / length)
    return ((jnp.cos(angle) + jnp.sin(angle)) * (1.0 / math.sqrt(length))).astype(jnp.bfloat16)


def slot_index(counts, capacity, radial):
    starts = jnp.cumsum(counts) - counts
    rows = jnp.arange(radial, dtype=jnp.int32)
    owner = jnp.sum((starts[None, :] <= rows[:, None]).astype(jnp.int32), axis=1) - 1
    return owner * capacity + rows - jnp.take(starts, owner)


def to_planes(values):
    return lax.all_to_all(values, "az", split_axis=3, concat_axis=0, tiled=True)


def to_modes(values):
    return lax.all_to_all(values, "az", split_axis=0, concat_axis=3, tiled=True)


def regroup_shells(values):
    return lax.all_to_all(values, "rad", split_axis=3, concat_axis=2, tiled=True)


def transform(cas_table, values):
    shape = values.shape
    flat = jnp.dot(cas_table, values.reshape(shape[0], -1), preferred_element_type=jnp.float32)
    return flat.astype(jnp.bfloat16).reshape(shape)


def plain_path(field, row_slot, cas_table, chosen_ids, radial_ops):
    chosen = jnp.take(radial_ops, chosen_ids, axis=0)
    gathered = to_planes(field)
    spectra = transform(cas_table, gathered)
    returned = to_modes(spectra)
    slab_data = regroup_shells(returned)
    packed = jnp.take(slab_data, row_slot, axis=2)
    result = jnp.einsum("crs,cfsx->cfxr", chosen, packed, preferred_element_type=jnp.float32)
    return result.astype(jnp.bfloat16)


def one_hot(flags):
    return jnp.where(flags, 1.0, 0.0).astype(jnp.bfloat16)


def grids(rows, columns):
    return (lax.broadcasted_iota(jnp.int32, (rows, columns), 0),
            lax.broadcasted_iota(jnp.int32, (rows, columns), 1))


def whole_kernel(n_az, n_rad, paired, field_ref, counts_ref, cas_ref, ops_ref, second_op_ref, out_ref,
                 raw, cells, shells, packed, planes_in, spectra, modes, results, turned_ops, pack,
                 rad_send, rad_recv, az_send, az_recv, back_send, back_recv, own_sem, raw_sem, out_sem,
                 beside=None, outgoing=None, near=None, rest=None, second=None,
                 pair_send=None, pair_recv=None):
    az, rad = lax.axis_index("az"), lax.axis_index("rad")
    chip, core = rad // 2, rad % 2
    _, fields, slab, planes, slots = cells.shape
    block = packed.shape[4]
    radial = n_az * block
    half = planes // 2
    parts = slab // PART
    chunks = fields * parts
    chips = range(n_rad // 2)

    def raw_copy(f):
        return pltpu.make_async_copy(field_ref.at[:, f], raw.at[f % 2], raw_sem.at[f])

    def out_copy(f):
        return pltpu.make_async_copy(results.at[f % 2], out_ref.at[:, f], out_sem.at[f])

    raw_copy(0).start()
    raw_copy(1).start()

    barrier = pltpu.get_barrier_semaphore()
    for step in range(1, n_rad):
        pl.semaphore_signal(barrier, inc=1, device_id=(az, lax.rem(rad + step, n_rad)), device_id_type=MESH)
    for step in range(1, n_az):
        pl.semaphore_signal(barrier, inc=1, device_id=(lax.rem(az + step, n_az), rad), device_id_type=MESH)

    def place(q):
        return q // parts, pl.ds((q % parts) * PART, PART)

    def halves(which):
        return pl.ds(pl.multiple_of(which * half, half), half)

    def pair_copy(q):
        f, here = place(q)
        return pltpu.make_async_remote_copy(
            src_ref=cells.at[:, f, here, halves(1 - core)], dst_ref=beside.at[q],
            send_sem=pair_send.at[q], recv_sem=pair_recv.at[q],
            device_id=(az, chip * 2 + 1 - core), device_id_type=MESH)

    def rad_ends(q, to):
        if paired:
            return outgoing.at[to, q], shells.at[chip, q, :, halves(core)]
        f, here = place(q)
        return cells.at[to, f, here], shells.at[rad, f, here]

    def rad_copy(q, step):
        other = lax.rem(rad + step, n_rad)
        source, target = rad_ends(q, other)
        return pltpu.make_async_remote_copy(
            src_ref=source, dst_ref=target,
            send_sem=rad_send.at[q, step], recv_sem=rad_recv.at[q, step],
            device_id=(az, other), device_id_type=MESH)

    def az_copy(q, step):
        f, here = place(q)
        other = lax.rem(az + step, n_az)
        return pltpu.make_async_remote_copy(
            src_ref=packed.at[f, other, here], dst_ref=planes_in.at[f, az, here],
            send_sem=az_send.at[q, step], recv_sem=az_recv.at[q, step],
            device_id=(other, rad), device_id_type=MESH)

    def back_copy(q, step):
        f, here = place(q)
        other = lax.rem(az + step, n_az)
        return pltpu.make_async_remote_copy(
            src_ref=spectra.at[f, other, here], dst_ref=modes.at[f, az, here],
            send_sem=back_send.at[q, step], recv_sem=back_recv.at[q, step],
            device_id=(other, rad), device_id_type=MESH)

    def own_shells(q):
        return pltpu.make_async_copy(*rad_ends(q, rad), own_sem.at[q, 0])

    def own_planes(q):
        f, here = place(q)
        return pltpu.make_async_copy(packed.at[f, az, here], planes_in.at[f, az, here], own_sem.at[q, 1])

    def own_spectra(q):
        f, here = place(q)
        return pltpu.make_async_copy(spectra.at[f, az, here], modes.at[f, az, here], own_sem.at[q, 2])

    rad_steps = range(1, n_rad)
    az_steps = range(1, n_az)

    def lay_out(f):
        raw_copy(f).wait()

        @pl.loop(0, planes // 16)
        def _(part):
            here = pl.ds(pl.multiple_of(part * 16, 16), 16)
            turned = jnp.swapaxes(raw[f % 2, here], 1, 2)
            by_cell = jnp.swapaxes(turned, 0, 1)
            cells[:, f, :, here, :] = by_cell.reshape(n_rad, slab, 16, slots)

    def start_rad(q):
        f, here = place(q)
        if paired:
            pair_copy(q).wait_recv()

            @pl.loop(0, n_rad // 4)
            def _(group):
                to = pl.ds(group * 4, 4)
                mine = cells[to, f, here, halves(core)].reshape(4 * PART * half, slots)
                both = jnp.concatenate([mine, beside[q, to].reshape(4 * PART * half, slots)], axis=1)
                close = jnp.dot(both, near[...], preferred_element_type=jnp.float32)
                outgoing[to, q, :PART] = close.astype(jnp.bfloat16).reshape(4, PART, half, slots)
                split = both.reshape(4, PART, half, 2 * slots)
                ends = [split[:, :PART // 2], split[:, PART // 2:]]
                ends = [end.reshape(4 * PART // 2 * half, 2 * slots) for end in ends]
                more = jnp.dot(jnp.concatenate(ends, axis=1), rest[...], preferred_element_type=jnp.float32)
                outgoing[to, q, PART:] = more.astype(jnp.bfloat16).reshape(4, PART // 2, half, slots)

        for step in rad_steps:
            rad_copy(q, step).start()
        own_shells(q).start()

    def dense_rows(q):
        f, here = place(q)
        if not paired:
            rows = [shells[j, f, here].reshape(PART * planes, slots) for j in range(n_rad)]
            return jnp.dot(jnp.concatenate(rows, axis=1), pack[...], preferred_element_type=jnp.float32)
        rows = [shells[j, q, :PART].reshape(PART * planes, slots) for j in chips]
        dense = jnp.dot(jnp.concatenate(rows, axis=1), pack[...], preferred_element_type=jnp.float32)
        rows = [shells[j, q, PART:].reshape(PART // 2 * planes, slots) for j in chips]
        rows = jnp.concatenate(rows, axis=1)
        more = [jnp.dot(rows, second[n], preferred_element_type=jnp.float32) for n in range(2)]
        return dense + jnp.concatenate(more, axis=0)

    def finish(q):
        f, _ = place(q)
        for step in az_steps:
            az_copy(q, step).wait_recv()
        own_planes(q).wait()

        @pl.loop(0, PART // 2)
        def _(pair):
            first = (q % parts) * PART + pair * 2
            both = [planes_in[f, :, first + x].reshape(n_az * planes, block) for x in range(2)]
            found = jnp.dot(cas_ref[...], jnp.concatenate(both, axis=1), preferred_element_type=jnp.float32)
            found = found.astype(jnp.bfloat16)
            for x in range(2):
                for k in range(n_az):
                    spectra[f, k, first + x] = found[k * planes:(k + 1) * planes, x * block:(x + 1) * block]

        for step in az_steps:
            back_copy(q, step).start()
        own_spectra(q).start()

    def apply_radial(f):
        @pl.loop(0, parts)
        def _(part):
            for step in az_steps:
                back_copy(f * parts + part, step).wait_recv()
            own_spectra(f * parts + part).wait()

        @pl.when(f >= 2)
        def _():
            out_copy(f - 2).wait()

        @pl.loop(0, planes // 16)
        def _(part):
            here = pl.ds(pl.multiple_of(part * 16, 16), 16)
            takes_second = second_op_ref[here]
            both = [[], []]
            for b in range(n_az):
                by_mode = jnp.swapaxes(modes[f, b, :, here], 0, 1)
                later = by_mode * takes_second
                both[0].append((by_mode - later).reshape(16 * slab, block))
                both[1].append(later.reshape(16 * slab, block))
            rows = jnp.concatenate(both[0] + both[1], axis=1)
            mapped = jnp.dot(rows, turned_ops[...], preferred_element_type=jnp.float32)
            results[f % 2, here] = mapped.astype(jnp.bfloat16).reshape(16, slab, radial)

        out_copy(f).start()

    counts = [counts_ref[j] for j in range(n_rad)]
    starts = [0 * counts[0]]
    for j in range(1, n_rad):
        starts.append(starts[-1] + counts[j - 1])

    if paired:
        row, column = grids(slots, slots)
        low = slots // 2
        mine, theirs = counts_ref[rad], counts_ref[chip * 2 + 1 - core]
        for n, (count, offset) in enumerate([(mine, core * theirs), (theirs, (1 - core) * mine)]):
            spot, held = row + offset, row < count
            near[n * slots:(n + 1) * slots, :] = one_hot((spot == column) & held)
            rest[n * slots:(n + 1) * slots, :] = one_hot((spot == slots + column) & held & (column < low))
            rest[(n + 2) * slots:(n + 3) * slots, :] = one_hot((spot == low + column) & held & (column >= low))

    lay_out(0)
    pl.semaphore_wait(barrier, n_rad + n_az - 2)
    if paired:
        for q in range(parts):
            pair_copy(q).start()

    @pl.loop(0, AHEAD)
    def _(q):
        start_rad(q)

    row, column = grids(slots, radial)
    if paired:
        for j in chips:
            begin, total, here = starts[2 * j], counts[2 * j] + counts[2 * j + 1], slice(j * slots, (j + 1) * slots)
            pack[here, :] = one_hot((row + begin == column) & (row < total))
            after = row + slots
            second[0, here, :] = one_hot((after + begin == column) & (after < total) & (row < low))
            after = row + low
            second[1, here, :] = one_hot((after + begin == column) & (after < total) & (row >= low))
    else:
        for j in range(n_rad):
            pack[j * slots:(j + 1) * slots, :] = one_hot((row + starts[j] == column) & (row < counts[j]))
    for n in range(2):
        turned_ops[n * radial:(n + 1) * radial, :] = ops_ref[n].T

    @pl.loop(0, chunks)
    def _(q):
        f, here = place(q)

        @pl.when((q % parts == 0) & (f + 1 < fields))
        def _():
            @pl.when(f + 2 < fields)
            def _():
                raw_copy(f + 2).start()

            lay_out(f + 1)
            if paired:
                for part in range(parts):
                    pair_copy(q + parts + part).start()

        @pl.when(q + AHEAD < chunks)
        def _():
            start_rad(q + AHEAD)

        for step in rad_steps:
            rad_copy(q, step).wait_recv()
        own_shells(q).wait()
        dense = dense_rows(q).astype(jnp.bfloat16)
        for k in range(n_az):
            packed[f, k, here] = dense[:, k * block:(k + 1) * block].reshape(PART, planes, block)

        for step in az_steps:
            az_copy(q, step).start()
        own_planes(q).start()

        @pl.when(q > 0)
        def _():
            finish(q - 1)

        @pl.when((q % parts == parts // 2) & (f > 0))
        def _():
            apply_radial(f - 1)

    finish(chunks - 1)
    apply_radial(fields - 1)

    @pl.loop(0, chunks)
    def _(q):
        if paired:
            pair_copy(q).wait_send()
        for step in rad_steps:
            rad_copy(q, step).wait_send()
        for step in az_steps:
            az_copy(q, step).wait_send()
            back_copy(q, step).wait_send()

    out_copy(fields - 2).wait()
    out_copy(fields - 1).wait()


def whole(field, shell_counts, cas_table, radial_ops, second_op, n_az, n_rad, paired):
    planes, fields, slots, length = field.shape
    slab = length // n_rad
    radial = radial_ops.shape[1]
    block = radial // n_az
    chunks = fields * slab // PART
    units = PART + PART // 2
    kind = field.dtype
    dma = pltpu.SemaphoreType.DMA
    spread = pltpu.VMEM((fields, n_az, slab, planes, block), kind)
    if paired:
        shells = pltpu.VMEM((n_rad // 2, chunks, units, planes, slots), kind)
        extra = [
            pltpu.VMEM((chunks, n_rad, PART, planes // 2, slots), kind),
            pltpu.VMEM((n_rad, chunks, units, planes // 2, slots), kind),
            pltpu.VMEM((2 * slots, slots), kind),
            pltpu.VMEM((4 * slots, slots), kind),
            pltpu.VMEM((2, n_rad // 2 * slots, radial), kind),
            dma((chunks,)), dma((chunks,)),
        ]
    else:
        shells = pltpu.VMEM((n_rad, fields, slab, planes, slots), kind)
        extra = []
    vmem = pl.BlockSpec(memory_space=pltpu.VMEM)
    return pl.pallas_call(
        functools.partial(whole_kernel, n_az, n_rad, paired),
        in_specs=[pl.BlockSpec(memory_space=pl.ANY), pl.BlockSpec(memory_space=pltpu.SMEM), vmem, vmem, vmem],
        out_specs=pl.BlockSpec(memory_space=pl.ANY),
        out_shape=jax.ShapeDtypeStruct((planes, fields, slab, radial), kind),
        scratch_shapes=[
            pltpu.VMEM((2, planes, slots, length), kind),
            pltpu.VMEM((n_rad, fields, slab, planes, slots), kind),
            shells, spread, spread, spread, spread,
            pltpu.VMEM((2, planes, slab, radial), kind),
            pltpu.VMEM((2 * radial, radial), kind),
            pltpu.VMEM((n_rad * slots // (2 if paired else 1), radial), kind),
            dma((chunks, n_rad)), dma((chunks, n_rad)),
            dma((chunks, n_az)), dma((chunks, n_az)),
            dma((chunks, n_az)), dma((chunks, n_az)),
            dma((chunks, 3)), dma((fields,)), dma((fields,)),
        ] + extra,
        compiler_params=pltpu.CompilerParams(
            collective_id=1 if paired else 0, has_side_effects=True, vmem_limit_bytes=VMEM_LIMIT),
    )(field, shell_counts, cas_table, radial_ops, second_op)


def per_device(field, shell_counts, op_index, radial_ops):
    planes, fields, slots, cells = field.shape
    n_az, n_rad = lax.axis_size("az"), lax.axis_size("rad")
    comps_all = planes * n_az
    radial = radial_ops.shape[1]
    cas_table = make_table(comps_all)
    comp_ids = lax.axis_index("az") * planes + jnp.arange(planes, dtype=jnp.int32)
    mode_ids = jnp.minimum(comp_ids, comps_all - comp_ids)
    slab = cells // n_rad
    if fields < 2 or slots % 128 or cells % 128 or n_rad % 4 or slab % 16 or planes % 32 or radial % (128 * n_az):
        row_slot = slot_index(shell_counts, slots, radial)
        return plain_path(field, row_slot, cas_table, jnp.take(op_index, mode_ids), radial_ops)
    numbers = jnp.arange(op_index.shape[0], dtype=jnp.int32)
    chosen_ids = jnp.sum(jnp.where(mode_ids[:, None] == numbers[None, :], op_index[None, :], 0), axis=1)
    second_op = jnp.broadcast_to(chosen_ids[:, None, None], (planes, slab, radial // n_az)).astype(field.dtype)
    chips = jnp.arange(n_rad, dtype=jnp.int32) // 2
    together = jnp.sum(jnp.where(chips[:, None] == chips[None, :], shell_counts[None, :], 0), axis=1)
    operands = (field, shell_counts, cas_table, radial_ops, second_op)
    return lax.cond(
        2 * jnp.max(together) <= 3 * slots,
        lambda *given: whole(*given, n_az, n_rad, True),
        lambda *given: whole(*given, n_az, n_rad, False),
        *operands)


def solution(mesh):
    return jax.shard_map(
        per_device,
        mesh=mesh,
        in_specs=(P("az", None, "rad", None), P(), P(), P()),
        out_specs=P("az", None, "rad", None),
        check_vma=False,
    )
```

time: 224 us -> 177 us (0.79)
  Pallas kernels: 216 us -> 164 us
  local copies, waits for them, and re-layouts: 0.72 us -> 5.85 us
    pallas_call x2 -> x1, Pallas kernels: 216 us -> 164 us  [whole(): pl.pallas_call(functools.partial(whole_kernel, n_az, n_rad, paired), in_s...]
    unnamed x0 -> x1, local copies, waits for them, and re-layouts: none -> 5.01 us
where the time goes in v4:
time: 177 us; the launch traced here: 174 us
  Pallas kernels  164 us (93%)
  local copies, waits for them, and re-layouts  5.85 us (3%)
  other arithmetic  3.44 us (2%)
    pallas_call x1, Pallas kernels, whole(): pl.pallas_call(functools.partial(whole_kernel, n_az, n_rad, paired), in_s...  164 us
    unnamed x1, local copies, waits for them, and re-layouts  5.01 us

profile of v4, /device:TPU:0, one launch (start us, length us, event | category | flops | bytes accessed | tf_op | source)
XLA Modules:
  0.0 173.6 jit_solution(11111147797227487780)
XLA Ops:
  0.0 0.9 select_reduce_fusion
  0.9 0.8 select_reduce_fusion.1
  1.7 0.6 reduce_max.9
  3.0 1.1 multiply_convert_fusion
  4.1 164.4 %conditional.1 = (bf16[64,4,16,512]{3,2,1,0:T(8,128)(2,1)}) conditional(s32[]{:T(128)} %convert_element_type.17, (bf16[64,4,128,128]{3,2,1,0:T(8,128)(2,1)}, s32[8]{0:T(128)}, bf16[256,256]{1,0:T(8,128)(2,1)S(1)}, bf16[2,512,512]{2,1,0:T(8,128)(2,1)}, bf16[64]{0:T(256)(128)(2,1)S(1)}) %tuple.11, (bf16[64,4,128,128]{3,2,1,0:T(8,128)(2,1)}, ...), branch_computations={%region_3.4_spmd, %region_4.5_spmd} | conditional | bytes 262280 | solution.py:406
  4.1 0.8 broadcast_in_dim.44.second_op_ref
  5.0 163.6 %branch_1_fun.1 = bf16[64,4,16,512]{3,2,1,0:T(8,128)(2,1)} custom-call(bf16[64,4,128,128]{3,2,1,0:T(8,128)(2,1)} %get-tuple-element.46.field_ref, s32[8]{0:T(128)} %get-tuple-element.34.counts_ref, bf16[256,256]{1,0:T(8,128)(2,1)S(1)} %get-tuple-element.35.cas_ref, bf16[2,512,512]{2,1,0:T(8,128)(2,1)} %get-tuple-element.48.ops_ref, ...), custom_call_target="tpu_custom_call" | custom-call | tf_op jit(solution)/shard_map/cond/branch_1_fun/pallas_call | solution.py:366
  168.6 5.0 %copy.14 = bf16[64,4,16,512]{3,2,1,0:T(8,128)(2,1)} copy(bf16[64,4,16,512]{3,2,1,0:T(8,128)(2,1)} %get-tuple-element.38) | data formatting | bytes 8388608
  (3 shorter events, 0.0 us)

commit v5 on v4

--- a/solution.py
+++ b/solution.py
@@ -11,7 +11,7 @@
 MESH = pl.DeviceIdType.MESH
 VMEM_LIMIT = 60 << 20
 PART = 4
-AHEAD = 2
+AHEAD = 1
 
 
 def make_table(length):
@@ -385,6 +385,23 @@
     )(field, shell_counts, cas_table, radial_ops, second_op)
 
 
+def hand_over_kernel(from_ref, to_ref):
+    to_ref[...] = from_ref[...]
+
+
+def hand_over(result):
+    block = (result.shape[0] // 4,) + result.shape[1:]
+    spec = pl.BlockSpec(block, lambda n: (n, 0, 0, 0))
+    return pl.pallas_call(
+        hand_over_kernel,
+        grid=(4,),
+        in_specs=[spec],
+        out_specs=spec,
+        out_shape=jax.ShapeDtypeStruct(result.shape, result.dtype),
+        compiler_params=pltpu.CompilerParams(vmem_limit_bytes=VMEM_LIMIT),
+    )(result)
+
+
 def per_device(field, shell_counts, op_index, radial_ops):
     planes, fields, slots, cells = field.shape
     n_az, n_rad = lax.axis_size("az"), lax.axis_size("rad")
@@ -403,11 +420,12 @@
     chips = jnp.arange(n_rad, dtype=jnp.int32) // 2
     together = jnp.sum(jnp.where(chips[:, None] == chips[None, :], shell_counts[None, :], 0), axis=1)
     operands = (field, shell_counts, cas_table, radial_ops, second_op)
-    return lax.cond(
+    result = lax.cond(
         2 * jnp.max(together) <= 3 * slots,
         lambda *given: whole(*given, n_az, n_rad, True),
         lambda *given: whole(*given, n_az, n_rad, False),
         *operands)
+    return hand_over(result)
 
 
 def solution(mesh):

time: 177 us -> 173 us (0.977); the launches traced: 174 us -> 173 us
  local copies, waits for them, and re-layouts: 5.85 us -> 0.13 us
  Pallas kernels: 164 us -> 168 us
    unnamed x1 -> x0, local copies, waits for them, and re-layouts: 5.01 us -> none
    pallas_call x0 -> x1, Pallas kernels: none -> 4.74 us  [hand_over(): pl.pallas_call(hand_over_kernel, grid=(4,), in_specs=[spec], out_specs=sp...]
where the time goes in v5:
time: 173 us
  Pallas kernels  168 us (97%)
  other arithmetic  3.44 us (2%)
    pallas_call x1, Pallas kernels, whole(): pl.pallas_call(functools.partial(whole_kernel, n_az, n_rad, paired), in_s...  164 us
    pallas_call x1, Pallas kernels, hand_over(): pl.pallas_call(hand_over_kernel, grid=(4,), in_specs=[spec], out_specs=sp...  4.74 us

profile of v5, /device:TPU:0, one launch (start us, length us, event | category | flops | bytes accessed | tf_op | source)
XLA Modules:
  0.0 172.7 jit_solution(4336422844627983058)
XLA Ops:
  0.0 0.9 select_reduce_fusion
  0.9 0.8 select_reduce_fusion.1
  1.7 0.6 reduce_max.9
  3.0 1.1 multiply_convert_fusion
  4.1 0.1 broadcast_in_dim.42
  4.3 163.7 %conditional.1 = (bf16[64,4,16,512]{3,2,1,0:T(8,128)(2,1)}) conditional(s32[]{:T(128)} %convert_element_type.17, (bf16[64,4,128,128]{3,2,1,0:T(8,128)(2,1)}, s32[8]{0:T(128)}, bf16[256,256]{1,0:T(8,128)(2,1)S(1)}, bf16[2,512,512]{2,1,0:T(8,128)(2,1)}, bf16[64,16,128]{2,1,0:T(8,128)(2,1)S(1)}) %tuple.11, (bf16[64,4,128,128]{3,2,1,0:T(8,128)(2,1)}, ...), branch_computations={%region_3.4_spmd, %region_4.5_spmd} | conditional | bytes 8 | solution.py:423
  4.3 163.7 %branch_1_fun.1 = bf16[64,4,16,512]{3,2,1,0:T(8,128)(2,1)} custom-call(bf16[64,4,128,128]{3,2,1,0:T(8,128)(2,1)} %get-tuple-element.33.field_ref, s32[8]{0:T(128)} %get-tuple-element.34.counts_ref, bf16[256,256]{1,0:T(8,128)(2,1)S(1)} %get-tuple-element.35.cas_ref, bf16[2,512,512]{2,1,0:T(8,128)(2,1)} %get-tuple-element.36.ops_ref, ...), custom_call_target="tpu_custom_call" | custom-call | tf_op jit(solution)/shard_map/cond/branch_1_fun/pallas_call | solution.py:366
  167.9 4.7 %shard_map.46 = bf16[64,4,16,512]{3,2,1,0:T(8,128)(2,1)} custom-call(bf16[64,4,16,512]{3,2,1,0:T(8,128)(2,1)} %get-tuple-element.38.from_ref), custom_call_target="tpu_custom_call" | custom-call | tf_op jit(solution)/shard_map/pallas_call | solution.py:395
  (3 shorter events, 0.0 us)

commit v6 on v5

--- a/solution.py
+++ b/solution.py
@@ -262,12 +262,16 @@
     lay_out(0)
     pl.semaphore_wait(barrier, n_rad + n_az - 2)
     if paired:
-        for q in range(parts):
+        for q in range(AHEAD):
             pair_copy(q).start()
 
     @pl.loop(0, AHEAD)
     def _(q):
         start_rad(q)
+
+    if paired:
+        for q in range(AHEAD, parts):
+            pair_copy(q).start()
 
     row, column = grids(slots, radial)
     if paired:

time: 173 us -> 173 us (level)
  no operation moved by 1% of the time
where the time goes in v6:
time: 173 us
  Pallas kernels  168 us (97%)
  other arithmetic  3.44 us (2%)
    pallas_call x1, Pallas kernels, whole(): pl.pallas_call(functools.partial(whole_kernel, n_az, n_rad, paired), in_s...  164 us
    pallas_call x1, Pallas kernels, hand_over(): pl.pallas_call(hand_over_kernel, grid=(4,), in_specs=[spec], out_specs=sp...  4.74 us

profile of v6, /device:TPU:0, one launch (start us, length us, event | category | flops | bytes accessed | tf_op | source)
XLA Modules:
  0.0 172.7 jit_solution(4529161937547130647)
XLA Ops:
  0.0 0.9 select_reduce_fusion
  0.9 0.8 select_reduce_fusion.1
  1.7 0.6 reduce_max.9
  3.0 1.1 multiply_convert_fusion
  4.1 0.1 broadcast_in_dim.42
  4.3 163.7 %conditional.1 = (bf16[64,4,16,512]{3,2,1,0:T(8,128)(2,1)}) conditional(s32[]{:T(128)} %convert_element_type.17, (bf16[64,4,128,128]{3,2,1,0:T(8,128)(2,1)}, s32[8]{0:T(128)}, bf16[256,256]{1,0:T(8,128)(2,1)S(1)}, bf16[2,512,512]{2,1,0:T(8,128)(2,1)}, bf16[64,16,128]{2,1,0:T(8,128)(2,1)S(1)}) %tuple.11, (bf16[64,4,128,128]{3,2,1,0:T(8,128)(2,1)}, ...), branch_computations={%region_3.4_spmd, %region_4.5_spmd} | conditional | bytes 8 | solution.py:427
  4.3 163.7 %branch_1_fun.1 = bf16[64,4,16,512]{3,2,1,0:T(8,128)(2,1)} custom-call(bf16[64,4,128,128]{3,2,1,0:T(8,128)(2,1)} %get-tuple-element.33.field_ref, s32[8]{0:T(128)} %get-tuple-element.34.counts_ref, bf16[256,256]{1,0:T(8,128)(2,1)S(1)} %get-tuple-element.35.cas_ref, bf16[2,512,512]{2,1,0:T(8,128)(2,1)} %get-tuple-element.36.ops_ref, ...), custom_call_target="tpu_custom_call" | custom-call | tf_op jit(solution)/shard_map/cond/branch_1_fun/pallas_call | solution.py:370
  168.0 4.7 %shard_map.46 = bf16[64,4,16,512]{3,2,1,0:T(8,128)(2,1)} custom-call(bf16[64,4,16,512]{3,2,1,0:T(8,128)(2,1)} %get-tuple-element.38.from_ref), custom_call_target="tpu_custom_call" | custom-call | tf_op jit(solution)/shard_map/pallas_call | solution.py:399
  (3 shorter events, 0.0 us)
